TPU v7x, 256 devices: a whole 4x4x8 slice. The times are simulated.
256 devices in a mesh: outer: 8 (over x, core), inner: 32 (over y, z).
Axes of the slice: x: 4, y: 4, z: 8, core: 2. Of those that a mesh axis runs over, the one named last changes fastest.
Arguments:
- basis: float32 [32768, 1024], P(('outer', 'inner')), may hold values from -0.1875 to 0.1875
- fields: float32 [32768, 64], P(('outer', 'inner')), may hold values from -6 to 6
- positions: int32 [32768], P(('outer', 'inner')), may hold values from 0 to 511
- nugget: float32 [32768], P(('outer', 'inner')), may hold values from 0.2 to 2
Outputs:
- posterior_mean: float32 [32768, 64], P(('outer', 'inner'))
- root_coef: float32 [512, 64], replicated
All inputs are finite; a program needn't handle non-finite values.
Results may differ from a plain program's by a relative error of at most 0.0001.
Values sent between devices are 32-bit elements; how exact they have to be, the bound alone decides.
A program may use at most 64 MiB of HBM per device.

v0:
```python
import functools

import jax
import jax.numpy as jnp
from jax import lax
from jax.experimental import pallas as pl
from jax.experimental.pallas import tpu as pltpu
from jax.sharding import Mesh
from jax.sharding import PartitionSpec as P

M = 512
R = 512
K = 1024
F = 64
RANGE = 8
B = 128
PIVOTS = 8
PANEL = 64
NB = M // B
OUTER_INNER = ("outer", "inner_0", "inner_1")
PAIRS = [(i, j) for i in range(NB) for j in range(i, NB)]
TRI = {pair: at for at, pair in enumerate(PAIRS)}
TRI_ROWS = len(PAIRS) * B
RED_ROWS = R // 2
TOP, REST, EARLY, LATE, ROOT = range(5)
PART_ROWS = {
    TOP: NB * B,
    REST: TRI_ROWS - NB * B,
    EARLY: (NB * NB // 2 + NB) * B,
    LATE: NB * NB // 2 * B,
    ROOT: TRI_ROWS,
}
Z_FIRST = (LATE,)


def dot(left, right, left_dim=1):
    return lax.dot_general(
        left,
        right,
        (((left_dim,), (0,)), ((), ())),
        precision=lax.Precision.HIGHEST,
        preferred_element_type=jnp.float32,
    )


def halves(x):
    high = x.astype(jnp.bfloat16)
    return high, (x - high.astype(jnp.float32)).astype(jnp.bfloat16)


def dot3(left, right, left_dim=1):
    left = left if isinstance(left, tuple) else halves(left)
    right = right if isinstance(right, tuple) else halves(right)

    def one(a, b):
        return lax.dot_general(
            a, b, (((left_dim,), (0,)), ((), ())), preferred_element_type=jnp.float32
        )

    return one(left[0], right[0]) + (one(left[0], right[1]) + one(left[1], right[0]))


def swept(block, n):
    def at(values, q, k):
        return values[(min(q, k), max(q, k))]

    for p in range(n):
        inverse = 1.0 / block[(p, p)]
        scaled = {q: at(block, q, p) * inverse for q in range(n) if q != p}
        new = {}
        for q in range(n):
            for k in range(q, n):
                if q == p and k == p:
                    new[(q, k)] = -inverse
                elif q == p:
                    new[(q, k)] = scaled[k]
                elif k == p:
                    new[(q, k)] = scaled[q]
                else:
                    new[(q, k)] = block[(q, k)] - scaled[q] * at(block, p, k)
        block = new
    return block


def tree_sum(terms):
    while len(terms) > 1:
        terms = [terms[i] + terms[i + 1] for i in range(0, len(terms), 2)]
    return terms[0]


def panel_rows(x):
    w, n = x.shape
    b = PIVOTS
    lane = lax.broadcasted_iota(jnp.int32, (b, n), 1)
    sub = lax.broadcasted_iota(jnp.int32, (b, n), 0)
    for p in range(0, w, b):
        inside = (lane >= p) & (lane < p + b)
        columns = [jnp.broadcast_to(x[:, p + k : p + k + 1], (w, n)) for k in range(b)]
        block = {
            (q, k): jnp.broadcast_to(columns[k][p + q : p + q + 1, :], (b, n))
            for q in range(b)
            for k in range(q, b)
        }
        minus_inverse = swept(block, b)
        top = jnp.where(inside, jnp.where(lane == sub + p, -1.0, 0.0), x[p : p + b, :])
        rows = [jnp.broadcast_to(top[k : k + 1, :], (b, n)) for k in range(b)]
        minus_new = [
            tree_sum([minus_inverse[(min(q, k), max(q, k))] * rows[k] for k in range(b)])
            for q in range(b)
        ]
        tiles = []
        for t in range(0, w, b):
            if t == p:
                tile = -minus_new[0]
                for q in range(1, b):
                    tile = jnp.where(sub == q, -minus_new[q], tile)
            else:
                tile = jnp.where(inside, 0.0, x[t : t + b, :]) + tree_sum(
                    [columns[k][t : t + b, :] * minus_new[k] for k in range(b)]
                )
            tiles.append(tile)
        x = jnp.concatenate(tiles, axis=0)
    return x


def half_swept(x):
    n = x.shape[0]
    new = panel_rows(x[0:PANEL, :])
    lane = lax.broadcasted_iota(jnp.int32, (n - PANEL, n), 1)
    rest = jnp.where(lane < PANEL, 0.0, x[PANEL:, :]) - dot(x[PANEL:, 0:PANEL], new)
    return pltpu.roll(jnp.concatenate([rest, new], axis=0), n - PANEL, 1)


def minus_inverse_of(x):
    return lax.fori_loop(0, x.shape[0] // PANEL, lambda _, held: half_swept(held), x)


def sweep_block(x_ref, new_ref, k):
    at = slice(k * B, (k + 1) * B)
    finish_block(x_ref, new_ref, k, minus_inverse_of(x_ref[at, at]))


def finish_block(x_ref, new_ref, k, minus):
    at = slice(k * B, (k + 1) * B)
    row = halves(x_ref[at, :])
    new_ref[...] = -dot3(minus, row)
    new_ref[:, at] = minus
    new = new_ref[...]
    right = halves(new)
    for i in range(NB):
        if i != k:
            rows = slice(i * B, (i + 1) * B)
            x_ref[rows, at] = jnp.zeros((B, B), jnp.float32)
            x_ref[rows, :] = x_ref[rows, :] - dot3(tuple(h[:, rows] for h in row), right, 0)
    x_ref[at, :] = new


def fill_symmetric(x_ref, row, blocks):
    diagonal = lax.broadcasted_iota(jnp.int32, (B, B), 0) == lax.broadcasted_iota(
        jnp.int32, (B, B), 1
    )
    eye = jnp.where(diagonal, 1.0, 0.0)
    for (i, j), at in TRI.items():
        if i not in row:
            continue
        value = blocks(at)
        ri, rj = slice(i * B, (i + 1) * B), slice(j * B, (j + 1) * B)
        if i == j:
            x_ref[ri, ri] = value + eye
        else:
            x_ref[ri, rj] = value
            x_ref[rj, ri] = value.T


def kernel(no, ny, nz, *refs):
    basis_ref, fields_ref, positions_ref, nugget_ref, mean_ref, root_ref = refs[:6]
    solved, padded = refs[6:8]
    local, first_in, held, second_in, full = (refs[8 + 5 * i : 13 + 5 * i] for i in range(5))
    knot, new_rows, weights, correction, outer_in, half_p, packed_p, root = refs[33:41]
    s1, r1, s2, r2, gs2, gr2, gs1, gr1, so, ro, psz, prz, psy, pry, psc, prc = refs[41:]
    o = lax.axis_index("outer")
    y = lax.axis_index("inner_0")
    z = lax.axis_index("inner_1")
    me = y * nz + z
    inner = ny * nz

    def y_peer(k):
        return {"inner_0": lax.rem(y + k, ny)}

    def z_peer(k):
        return {"inner_1": lax.rem(z + k, nz)}

    def o_peer(k):
        return {"outer": lax.rem(o + k, no)}

    def axes(part):
        in_y, in_z = (ny, y, y_peer), (nz, z, z_peer)
        return (in_z, in_y) if part in Z_FIRST else (in_y, in_z)

    peers = (
        [y_peer(k) for k in range(1, ny)]
        + [z_peer(k) for k in range(1, nz)]
        + [o_peer(k) for k in range(1, no)]
    )
    barrier = pltpu.get_barrier_semaphore()
    for peer in peers:
        pl.semaphore_signal(barrier, inc=1, device_id=peer, device_id_type=pl.DeviceIdType.MESH)

    sent = []

    def send(src, dst, send_sem, recv_sem, peer):
        copy = pltpu.make_async_remote_copy(
            src_ref=src,
            dst_ref=dst,
            send_sem=send_sem,
            recv_sem=recv_sem,
            device_id=peer,
            device_id_type=pl.DeviceIdType.MESH,
        )
        copy.start()
        sent.append(copy)
        return copy

    def span(index, rows):
        return pl.ds(pl.multiple_of(index * rows, 8), rows)

    def own(part):
        (n1, i1, _), (n2, i2, _) = axes(part)
        return span(i1 * n2 + i2, PART_ROWS[part] // inner)

    def summed(landing, mine):
        total = mine
        for k in range(landing.shape[0]):
            total = total + landing[k]
        return total

    def arrived(copies):
        for copy in copies:
            copy.wait_recv()

    pending = {}

    def sum_first(part):
        n, index, peer = axes(part)[0]
        rows = PART_ROWS[part] // n
        pending[part] = [
            send(
                local[part].at[span(lax.rem(index + k, n), rows)],
                first_in[part].at[k - 1],
                s1.at[part, k - 1],
                r1.at[part, k - 1],
                peer(k),
            )
            for k in range(1, n)
        ]

    def sum_second(part):
        n1, index1, _ = axes(part)[0]
        n, index, peer = axes(part)[1]
        arrived(pending[part])
        held[part][...] = summed(
            first_in[part], local[part][span(index1, PART_ROWS[part] // n1), :]
        )
        rows = PART_ROWS[part] // inner
        pending[part] = [
            send(
                held[part].at[span(lax.rem(index + k, n), rows)],
                second_in[part].at[k - 1],
                s2.at[part, k - 1],
                r2.at[part, k - 1],
                peer(k),
            )
            for k in range(1, n)
        ]

    def whole_sum(part):
        _, index, _ = axes(part)[1]
        arrived(pending[part])
        return summed(second_in[part], held[part][span(index, PART_ROWS[part] // inner), :])

    def gather_second(part):
        full[part][own(part), :] = whole_sum(part)
        n, _, peer = axes(part)[1]
        block = full[part].at[own(part)]
        pending[part] = [
            send(block, block, gs2.at[part, k - 1], gr2.at[part, k - 1], peer(k))
            for k in range(1, n)
        ]

    def gather_first(part):
        arrived(pending[part])
        n, index, peer = axes(part)[0]
        block = full[part].at[span(index, PART_ROWS[part] // n)]
        pending[part] = [
            send(block, block, gs1.at[part, k - 1], gr1.at[part, k - 1], peer(k))
            for k in range(1, n)
        ]

    def gathered(part):
        arrived(pending[part])

    def basis_block(i):
        return basis_ref[:, i * B : (i + 1) * B]

    def cross(ref_early, ref_late, k, j):
        block = k * NB + j
        late = block - NB * NB // 2
        ref, at = (ref_late, late) if late >= 0 else (ref_early, block)
        return ref.at[at * B : (at + 1) * B]

    def rhs(ref_early, k):
        at = NB * NB // 2 + k
        return ref_early.at[at * B : (at + 1) * B]

    position = jnp.broadcast_to(positions_ref[...].astype(jnp.float32), (B, B))
    diagonal = lax.broadcasted_iota(jnp.int32, (B, B), 0) == lax.broadcasted_iota(
        jnp.int32, (B, B), 1
    )
    covariance = jnp.exp(-jnp.abs(position - position.T) / RANGE) + jnp.where(
        diagonal, jnp.broadcast_to(nugget_ref[...], (B, B)), 0.0
    )
    minus = minus_inverse_of(covariance)
    solved[:, 0:M] = -dot3(minus, basis_ref[:, 0:M])
    row = dot3(basis_block(0), solved[:, 0:M], 0)
    for j in range(NB):
        local[TOP][j * B : (j + 1) * B, :] = row[:, j * B : (j + 1) * B]
    pl.semaphore_wait(barrier, len(peers))
    sum_first(TOP)
    for i in range(1, NB):
        row = dot3(basis_block(i), solved[:, i * B : M], 0)
        for j in range(i, NB):
            at = (TRI[(i, j)] - NB) * B
            local[REST][at : at + B, :] = row[:, (j - i) * B : (j - i + 1) * B]
    sum_first(REST)
    solved[:, M:] = -dot3(minus, basis_ref[:, M:])
    padded[...] = jnp.zeros_like(padded)
    padded[:, 0:F] = fields_ref[...]
    left_fields = -dot3(minus, padded[...])
    right_fields = pltpu.roll(left_fields, F, 1)

    def cross_rows(k):
        row = dot3(basis_block(k), solved[:, M:], 0)
        for j in range(NB):
            cross(local[EARLY], local[LATE], k, j)[...] = row[:, j * B : (j + 1) * B]

    for k in range(NB // 2):
        cross_rows(k)
    for i in range(NB):
        rhs(local[EARLY], i)[...] = dot3(basis_block(i), left_fields, 0) + dot3(
            basis_block(NB + i), right_fields, 0
        )
    sum_second(TOP)
    for k in range(NB // 2, NB):
        cross_rows(k)
    gather_second(TOP)
    sum_second(REST)
    gather_first(TOP)
    for i in range(NB):
        row = dot3(basis_block(NB + i), solved[:, M + i * B :], 0)
        for j in range(i, NB):
            at = TRI[(i, j)] * B
            local[ROOT][at : at + B, :] = row[:, (j - i) * B : (j - i + 1) * B]
    gather_second(REST)
    gathered(TOP)
    gather_first(REST)
    sum_first(EARLY)
    sum_first(LATE)

    fill_symmetric(knot, (0,), lambda at: full[TOP][at * B : (at + 1) * B, :])
    minus = half_swept(knot[0:B, 0:B])
    minus = half_swept(minus)
    gathered(REST)
    fill_symmetric(
        knot, (1, 2, 3), lambda at: full[REST][(at - NB) * B : (at - NB + 1) * B, :]
    )
    finish_block(knot, new_rows, 0, minus)
    minus = half_swept(knot[B : 2 * B, B : 2 * B])
    sum_second(EARLY)
    sum_second(LATE)
    minus = half_swept(minus)
    finish_block(knot, new_rows, 1, minus)
    gather_second(EARLY)
    gather_second(LATE)
    minus = half_swept(knot[2 * B : 3 * B, 2 * B : 3 * B])
    gather_first(LATE)
    gather_first(EARLY)
    sum_first(ROOT)
    minus = half_swept(minus)
    finish_block(knot, new_rows, 2, minus)
    minus = half_swept(knot[3 * B :, 3 * B :])
    sum_second(ROOT)
    minus = half_swept(minus)
    finish_block(knot, new_rows, 3, minus)
    gathered(EARLY)
    gathered(LATE)

    def cross_at(k, j):
        return cross(full[EARLY], full[LATE], k, j)[...]

    def rhs_at(k):
        return rhs(full[EARLY], k)[...]

    right = halves(
        jnp.concatenate(
            [
                jnp.concatenate([cross_at(k, j) for j in range(NB)] + [rhs_at(k)], axis=1)
                for k in range(NB)
            ],
            axis=0,
        )
    )
    weights[...] = -dot3(knot[...], right)
    solved_cross = halves(weights[...])
    reduced = []
    for i in range(NB):
        total = dot3(
            tuple(h[:, i * B : (i + 1) * B] for h in right),
            tuple(h[:, i * B :] for h in solved_cross),
            0,
        )
        for j in range(i, NB):
            at = TRI[(i, j)] * B
            correction[at : at + B, :] = total[:, (j - i) * B : (j - i + 1) * B]
        reduced.append(pltpu.roll(rhs_at(i), F, 1) - total[:, (NB - i) * B :])
    lane = lax.broadcasted_iota(jnp.int32, (B, B), 1)
    for i in range(NB // 2):
        at = TRI_ROWS + i * B
        correction[at : at + B, :] = jnp.where(
            lane < F, reduced[i], pltpu.roll(reduced[i + NB // 2], F, 1)
        )
    a_share, r_share = TRI_ROWS // inner, RED_ROWS // inner
    share = a_share + r_share
    outer_in[o, 0:a_share, :] = whole_sum(ROOT) - correction[span(me, a_share), :]
    outer_in[o, a_share:share, :] = correction[
        pl.ds(pl.multiple_of(TRI_ROWS + me * r_share, 8), r_share), :
    ]
    arrived(
        [
            send(outer_in.at[o], outer_in.at[o], so.at[k - 1], ro.at[k - 1], o_peer(k))
            for k in range(1, no)
        ]
    )

    core = lax.rem(o, 2)
    sibling = {"outer": o + 1 - 2 * core}
    h = share // 2
    mine = pl.ds(pl.multiple_of(core * h, 8), h)
    total = outer_in[0, mine, :]
    for k in range(1, no):
        total = total + outer_in[k, mine, :]
    half_p[core, span(me, h), :] = total
    block = half_p.at[core, span(me, h)]
    arrived(
        [
            send(block, block, psz.at[k - 1], prz.at[k - 1], z_peer(k))
            for k in range(1, nz)
        ]
    )
    block = half_p.at[core, span(y, h * nz)]
    over_y = [
        send(block, block, psy.at[k - 1], pry.at[k - 1], y_peer(k)) for k in range(1, ny)
    ]
    swaps = [send(block, block, psc.at[0], prc.at[0], sibling)]
    for k in range(1, ny):
        over_y[k - 1].wait_recv()
        block = half_p.at[core, span(lax.rem(y + ny - k, ny), h * nz)]
        swaps.append(send(block, block, psc.at[k], prc.at[k], sibling))
    arrived(swaps)
    for d in range(inner):
        for c in range(2):
            lo, hi = c * h, min((c + 1) * h, a_share)
            packed_p[d * a_share + lo : d * a_share + hi, :] = half_p[
                c, d * h : d * h + hi - lo, :
            ]
        at = TRI_ROWS + d * r_share
        packed_p[at : at + r_share, :] = half_p[1, (d + 1) * h - r_share : (d + 1) * h, :]

    fill_symmetric(root, range(NB), lambda at: packed_p[at * B : (at + 1) * B, :])
    for k in range(NB):
        sweep_block(root, new_rows, k)
    half = packed_p[TRI_ROWS:, :]
    root_coef = -dot3(root[...], jnp.concatenate([half, pltpu.roll(half, F, 1)], axis=0))
    root_ref[...] = root_coef[:, 0:F]
    region_coef = weights[:, M:] - dot3(weights[:, 0:M], root_coef)
    mean = dot3(basis_ref[:, 0:M], region_coef) + dot3(basis_ref[:, M:], root_coef)
    mean_ref[...] = mean[:, 0:F]
    for copy in sent:
        copy.wait_send()


def shards(basis, fields, positions, nugget):
    no, ny, nz = (lax.axis_size(axis) for axis in OUTER_INNER)
    inner = ny * nz
    f32 = jnp.float32

    def landing(parts, rows):
        return pltpu.VMEM((parts, rows, B), f32)

    def flat(rows):
        return pltpu.VMEM((rows, B), f32)

    share = (TRI_ROWS + RED_ROWS) // inner
    dma = pltpu.SemaphoreType.DMA
    parts = list(PART_ROWS.items())
    first = [nz if part in Z_FIRST else ny for part, _ in parts]
    widest = max(ny, nz) - 1
    scratch = (
        [pltpu.VMEM((B, K), f32), flat(B)]
        + [flat(rows) for _, rows in parts]
        + [landing(n - 1, rows // n) for n, (_, rows) in zip(first, parts)]
        + [flat(rows // n) for n, (_, rows) in zip(first, parts)]
        + [landing(inner // n - 1, rows // inner) for n, (_, rows) in zip(first, parts)]
        + [flat(rows if part != ROOT else B) for part, rows in parts]
        + [pltpu.VMEM((M, M), f32), pltpu.VMEM((B, M), f32), pltpu.VMEM((M, M + B), f32)]
        + [flat(TRI_ROWS + RED_ROWS), landing(no, share), landing(2, share // 2 * inner)]
        + [flat(TRI_ROWS + RED_ROWS), pltpu.VMEM((R, R), f32)]
        + [dma((len(parts), widest))] * 8
        + [dma((no - 1,))] * 2
        + [dma((nz - 1,))] * 2
        + [dma((ny - 1,))] * 2
        + [dma((ny,))] * 2
    )
    return pl.pallas_call(
        functools.partial(kernel, no, ny, nz),
        out_shape=(
            jax.ShapeDtypeStruct((B, F), f32),
            jax.ShapeDtypeStruct((R, F), f32),
        ),
        in_specs=[pl.BlockSpec(memory_space=pltpu.VMEM)] * 4,
        out_specs=(pl.BlockSpec(memory_space=pltpu.VMEM),) * 2,
        scratch_shapes=scratch,
        compiler_params=pltpu.CompilerParams(
            collective_id=0, has_side_effects=True, vmem_limit_bytes=48 * 1024 * 1024
        ),
    )(basis, fields, positions.reshape(1, B), nugget.reshape(1, B))


def solution(mesh):
    split = Mesh(mesh.devices.reshape(mesh.shape["outer"], 4, 8), ("outer", "inner_0", "inner_1"))
    in_specs = (P(OUTER_INNER, None), P(OUTER_INNER, None), P(OUTER_INNER), P(OUTER_INNER))
    out_specs = (P(OUTER_INNER, None), P())
    return jax.shard_map(
        shards, mesh=split, in_specs=in_specs, out_specs=out_specs, check_vma=False
    )
```

profile of v0, /device:TPU:1, one launch (start us, length us, event | category | flops | bytes accessed | tf_op | source)
XLA Modules:
  0.0 136.1 jit_solution(11634079441585699680)
XLA Ops:
  0.6 0.0 copy-start.1
  0.6 0.0 copy-start.2
  0.7 0.9 copy.6.refs_1_
  1.5 0.0 copy-done.1
  1.5 0.0 copy-done.2
  1.5 0.0 copy-start
  1.5 1.0 copy-done
  2.6 132.0 %shard_map.59 = (f32[128,64]{1,0:T(8,128)S(1)}, f32[512,64]{1,0:T(8,128)S(1)}) custom-call(f32[128,1024]{1,0:T(8,128)S(1)} %copy-done, f32[128,64]{1,0:T(8,128)S(1)} %copy.6.refs_1_, s32[1,128]{1,0:T(1,128)S(1)} %bitcast.2, f32[1,128]{1,0:T(1,128)S(1)} %bitcast.3), custom_call_target="tpu_custom_call" | custom-call | tf_op jit(solution)/shard_map/pallas_call | solution.py:523
  134.6 0.7 copy.7
  135.3 0.8 copy.8
Async XLA Ops:
  0.6 0.9 copy-start.1
  0.6 0.9 copy-start.2
  1.5 1.0 copy-start
where the time goes:
time: 136 us
  Pallas kernels  132 us (97%)
  local copies, waits for them, and re-layouts  3.37 us (2%)
    pallas_call x1, Pallas kernels, shards(): pl.pallas_call(functools.partial(kernel, no, ny, nz), out_shape=(jax.Shap...  132 us

commit v1 on v0

--- a/solution.py
+++ b/solution.py
@@ -350,6 +350,7 @@
             basis_block(NB + i), right_fields, 0
         )
     sum_second(TOP)
+    sum_first(EARLY)
     for k in range(NB // 2, NB):
         cross_rows(k)
     gather_second(TOP)
@@ -361,13 +362,14 @@
             at = TRI[(i, j)] * B
             local[ROOT][at : at + B, :] = row[:, (j - i) * B : (j - i + 1) * B]
     gather_second(REST)
+    sum_first(LATE)
     gathered(TOP)
-    gather_first(REST)
-    sum_first(EARLY)
-    sum_first(LATE)
 
     fill_symmetric(knot, (0,), lambda at: full[TOP][at * B : (at + 1) * B, :])
     minus = half_swept(knot[0:B, 0:B])
+    gather_first(REST)
+    sum_second(EARLY)
+    sum_first(ROOT)
     minus = half_swept(minus)
     gathered(REST)
     fill_symmetric(
@@ -375,20 +377,18 @@
     )
     finish_block(knot, new_rows, 0, minus)
     minus = half_swept(knot[B : 2 * B, B : 2 * B])
-    sum_second(EARLY)
     sum_second(LATE)
+    gather_second(EARLY)
     minus = half_swept(minus)
     finish_block(knot, new_rows, 1, minus)
-    gather_second(EARLY)
     gather_second(LATE)
+    gather_first(EARLY)
     minus = half_swept(knot[2 * B : 3 * B, 2 * B : 3 * B])
     gather_first(LATE)
-    gather_first(EARLY)
-    sum_first(ROOT)
+    sum_second(ROOT)
     minus = half_swept(minus)
     finish_block(knot, new_rows, 2, minus)
     minus = half_swept(knot[3 * B :, 3 * B :])
-    sum_second(ROOT)
     minus = half_swept(minus)
     finish_block(knot, new_rows, 3, minus)
     gathered(EARLY)

time: 136 us -> 123 us (0.904)
  Pallas kernels: 132 us -> 119 us
    pallas_call x1, Pallas kernels: 132 us -> 119 us  [shards(): pl.pallas_call(functools.partial(kernel, no, ny, nz), out_shape=(jax.Shap...]
where the time goes in v1:
time: 123 us
  Pallas kernels  119 us (97%)
  local copies, waits for them, and re-layouts  3.37 us (3%)
    pallas_call x1, Pallas kernels, shards(): pl.pallas_call(functools.partial(kernel, no, ny, nz), out_shape=(jax.Shap...  119 us

profile of v1, /device:TPU:1, one launch (start us, length us, event | category | flops | bytes accessed | tf_op | source)
XLA Modules:
  0.0 122.6 jit_solution(14125436130364509802)
XLA Ops:
  0.6 0.0 copy-start.1
  0.6 0.0 copy-start.2
  0.7 0.9 copy.6.refs_1_
  1.5 0.0 copy-done.1
  1.5 0.0 copy-done.2
  1.5 0.0 copy-start
  1.5 1.0 copy-done
  2.6 118.5 %shard_map.59 = (f32[128,64]{1,0:T(8,128)S(1)}, f32[512,64]{1,0:T(8,128)S(1)}) custom-call(f32[128,1024]{1,0:T(8,128)S(1)} %copy-done, f32[128,64]{1,0:T(8,128)S(1)} %copy.6.refs_1_, s32[1,128]{1,0:T(1,128)S(1)} %bitcast.2, f32[1,128]{1,0:T(1,128)S(1)} %bitcast.3), custom_call_target="tpu_custom_call" | custom-call | tf_op jit(solution)/shard_map/pallas_call | solution.py:523
  121.1 0.7 copy.7
  121.8 0.8 copy.8
Async XLA Ops:
  0.6 0.9 copy-start.1
  0.6 0.9 copy-start.2
  1.5 1.0 copy-start

commit v2 on v1

--- a/solution.py
+++ b/solution.py
@@ -173,11 +173,18 @@
 
 
 def kernel(no, ny, nz, *refs):
-    basis_ref, fields_ref, positions_ref, nugget_ref, mean_ref, root_ref = refs[:6]
+    basis_far, fields_far, positions_ref, nugget_ref, mean_ref, root_ref = refs[:6]
     solved, padded = refs[6:8]
     local, first_in, held, second_in, full = (refs[8 + 5 * i : 13 + 5 * i] for i in range(5))
     knot, new_rows, weights, correction, outer_in, half_p, packed_p, root = refs[33:41]
-    s1, r1, s2, r2, gs2, gr2, gs1, gr1, so, ro, psz, prz, psy, pry, psc, prc = refs[41:]
+    s1, r1, s2, r2, gs2, gr2, gs1, gr1, so, ro, psz, prz, psy, pry, psc, prc = refs[41:57]
+    basis_ref, fields_ref, loaded = refs[57:]
+    loads = [
+        pltpu.make_async_copy(basis_far, basis_ref, loaded.at[0]),
+        pltpu.make_async_copy(fields_far, fields_ref, loaded.at[1]),
+    ]
+    for load in loads:
+        load.start()
     o = lax.axis_index("outer")
     y = lax.axis_index("inner_0")
     z = lax.axis_index("inner_1")
@@ -320,6 +327,8 @@
         diagonal, jnp.broadcast_to(nugget_ref[...], (B, B)), 0.0
     )
     minus = minus_inverse_of(covariance)
+    for load in loads:
+        load.wait()
     solved[:, 0:M] = -dot3(minus, basis_ref[:, 0:M])
     row = dot3(basis_block(0), solved[:, 0:M], 0)
     for j in range(NB):
@@ -334,8 +343,8 @@
     sum_first(REST)
     solved[:, M:] = -dot3(minus, basis_ref[:, M:])
     padded[...] = jnp.zeros_like(padded)
-    padded[:, 0:F] = fields_ref[...]
-    left_fields = -dot3(minus, padded[...])
+    padded[0:F, :] = fields_ref[...]
+    left_fields = -dot3(minus, padded[...].T)
     right_fields = pltpu.roll(left_fields, F, 1)
 
     def cross_rows(k):
@@ -376,40 +385,41 @@
         knot, (1, 2, 3), lambda at: full[REST][(at - NB) * B : (at - NB + 1) * B, :]
     )
     finish_block(knot, new_rows, 0, minus)
-    minus = half_swept(knot[B : 2 * B, B : 2 * B])
     sum_second(LATE)
     gather_second(EARLY)
+    minus = half_swept(knot[B : 2 * B, B : 2 * B])
+    gather_second(LATE)
+    gather_first(EARLY)
     minus = half_swept(minus)
     finish_block(knot, new_rows, 1, minus)
-    gather_second(LATE)
-    gather_first(EARLY)
-    minus = half_swept(knot[2 * B : 3 * B, 2 * B : 3 * B])
     gather_first(LATE)
     sum_second(ROOT)
-    minus = half_swept(minus)
-    finish_block(knot, new_rows, 2, minus)
-    minus = half_swept(knot[3 * B :, 3 * B :])
-    minus = half_swept(minus)
-    finish_block(knot, new_rows, 3, minus)
-    gathered(EARLY)
-    gathered(LATE)
-
+    for k in range(2, NB):
+        sweep_block(knot, new_rows, k)
     def cross_at(k, j):
         return cross(full[EARLY], full[LATE], k, j)[...]
 
     def rhs_at(k):
         return rhs(full[EARLY], k)[...]
 
-    right = halves(
-        jnp.concatenate(
-            [
-                jnp.concatenate([cross_at(k, j) for j in range(NB)] + [rhs_at(k)], axis=1)
-                for k in range(NB)
-            ],
-            axis=0,
-        )
-    )
-    weights[...] = -dot3(knot[...], right)
+    def rows_of(ks):
+        return halves(
+            jnp.concatenate(
+                [
+                    jnp.concatenate([cross_at(k, j) for j in range(NB)] + [rhs_at(k)], axis=1)
+                    for k in ks
+                ],
+                axis=0,
+            )
+        )
+
+    gathered(EARLY)
+    upper = rows_of(range(NB // 2))
+    weights[...] = -dot3(knot[:, 0 : M // 2], upper)
+    gathered(LATE)
+    lower = rows_of(range(NB // 2, NB))
+    weights[...] = weights[...] - dot3(knot[:, M // 2 :], lower)
+    right = tuple(jnp.concatenate(pair, axis=0) for pair in zip(upper, lower))
     solved_cross = halves(weights[...])
     reduced = []
     for i in range(NB):
@@ -480,10 +490,11 @@
         sweep_block(root, new_rows, k)
     half = packed_p[TRI_ROWS:, :]
     root_coef = -dot3(root[...], jnp.concatenate([half, pltpu.roll(half, F, 1)], axis=0))
-    root_ref[...] = root_coef[:, 0:F]
+    for i in range(NB):
+        root_ref[:, i * B : (i + 1) * B] = root_coef[i * B : (i + 1) * B, :].T[0:F, :]
     region_coef = weights[:, M:] - dot3(weights[:, 0:M], root_coef)
     mean = dot3(basis_ref[:, 0:M], region_coef) + dot3(basis_ref[:, M:], root_coef)
-    mean_ref[...] = mean[:, 0:F]
+    mean_ref[...] = mean.T[0:F, :]
     for copy in sent:
         copy.wait_send()
 
@@ -519,20 +530,23 @@
         + [dma((nz - 1,))] * 2
         + [dma((ny - 1,))] * 2
         + [dma((ny,))] * 2
-    )
-    return pl.pallas_call(
+        + [pltpu.VMEM((B, K), f32), pltpu.VMEM((F, B), f32), dma((2,))]
+    )
+    mean, root_coef = pl.pallas_call(
         functools.partial(kernel, no, ny, nz),
         out_shape=(
-            jax.ShapeDtypeStruct((B, F), f32),
-            jax.ShapeDtypeStruct((R, F), f32),
+            jax.ShapeDtypeStruct((F, B), f32),
+            jax.ShapeDtypeStruct((F, R), f32),
         ),
-        in_specs=[pl.BlockSpec(memory_space=pltpu.VMEM)] * 4,
+        in_specs=[pl.BlockSpec(memory_space=pltpu.HBM)] * 2
+        + [pl.BlockSpec(memory_space=pltpu.VMEM)] * 2,
         out_specs=(pl.BlockSpec(memory_space=pltpu.VMEM),) * 2,
         scratch_shapes=scratch,
         compiler_params=pltpu.CompilerParams(
-            collective_id=0, has_side_effects=True, vmem_limit_bytes=48 * 1024 * 1024
+            collective_id=0, has_side_effects=True, vmem_limit_bytes=60 * 1024 * 1024
         ),
-    )(basis, fields, positions.reshape(1, B), nugget.reshape(1, B))
+    )(basis, fields.T, positions.reshape(1, B), nugget.reshape(1, B))
+    return mean.T, root_coef.T
 
 
 def solution(mesh):

time: 123 us -> 122 us (level)
    pallas_call x2 -> x0, local copies, waits for them, and re-layouts: 1.47 us -> none  [shards(): pl.pallas_call(functools.partial(kernel, no, ny, nz), out_shape=(jax.Shap...]
    unnamed x7 -> x2, local copies, waits for them, and re-layouts: 1.9 us -> 2.94 us
where the time goes in v2:
time: 122 us
  Pallas kernels  119 us (98%)
  local copies, waits for them, and re-layouts  2.94 us (2%)
    pallas_call x1, Pallas kernels, shards(): pl.pallas_call(functools.partial(kernel, no, ny, nz), out_shape=(jax.Shap...  119 us
    unnamed x2, local copies, waits for them, and re-layouts  2.94 us

profile of v2, /device:TPU:1, one launch (start us, length us, event | category | flops | bytes accessed | tf_op | source)
XLA Modules:
  0.0 122.2 jit_solution(10487836420002854839)
XLA Ops:
  0.6 118.7 %shard_map.59 = (f32[64,128]{1,0:T(8,128)}, f32[64,512]{1,0:T(8,128)}) custom-call(f32[128,1024]{1,0:T(8,128)} %refs_0_.1, f32[64,128]{1,0:T(8,128)} %bitcast.6, s32[1,128]{1,0:T(1,128)} %bitcast.8, f32[1,128]{1,0:T(1,128)} %bitcast.9), custom_call_target="tpu_custom_call" | custom-call | tf_op jit(solution)/shard_map/pallas_call | solution.py:535
  119.3 1.4 %copy.8 = f32[128,64]{0,1:T(8,128)} copy(f32[128,64]{0,1:T(8,128)} %bitcast.7) | data formatting | bytes 65536
  120.7 1.6 %copy.9 = f32[512,64]{0,1:T(8,128)} copy(f32[512,64]{0,1:T(8,128)} %bitcast.5) | data formatting | bytes 262144
